TPU v7x, 128 devices: a whole 4x4x4 slice. The times are simulated.
128 devices in a mesh: row: 8 (over z, y_lo), col: 16 (over y_hi, x, core).
Axes of the slice: x: 4, y: 4 (y_hi: 2, y_lo: 2; y = y_hi * 2 + y_lo), z: 4, core: 2. Of those that a mesh axis runs over, the one named last changes fastest.
Arguments:
- hidden: bfloat16 [2048, 26624], P('col', 'row'), may hold values from -6 to 6
- weight: bfloat16 [26624, 8192], P('row', 'col'), may hold values from -0.0546875 to 0.0546875
- grad_out: bfloat16 [2048, 8192], P('row', 'col'), may hold values from -6 to 6
Outputs:
- output: bfloat16 [2048, 8192], P('row', 'col')
- grad_hidden: bfloat16 [2048, 26624], P('col', 'row')
- grad_weight: bfloat16 [26624, 8192], P('row', 'col')
All inputs are finite; a program needn't handle non-finite values.
Results may differ from a plain program's by a relative error of at most 0.019.
Values may be sent and summed in bfloat16 or wider, within the bound.
No kernel may reach another device: no remote copies, remote signals or barrier semaphores. Data moves between devices by JAX's collectives and lax.ppermute only.
A program may use at most 128 MiB of HBM per device.

v0:
```python
import jax
import jax.numpy as jnp
from jax import lax
from jax.sharding import PartitionSpec as P


def per_device(hidden, weight, grad_out):
    cotangents = lax.all_gather(grad_out, "row", axis=0, tiled=True)
    gathered = lax.all_gather(hidden, "col", axis=0, tiled=True)
    partial_out = jnp.dot(gathered, weight, preferred_element_type=jnp.float32)
    grad_weight = lax.dot_general(
        gathered, cotangents, (((0,), (0,)), ((), ())), preferred_element_type=jnp.float32
    )
    output = lax.psum_scatter(
        partial_out.astype(jnp.bfloat16), "row", scatter_dimension=0, tiled=True
    )
    part = lax.dot_general(
        cotangents, weight, (((1,), (1,)), ((), ())), preferred_element_type=jnp.float32
    )
    part = lax.optimization_barrier(part.astype(jnp.bfloat16))
    grad_hidden = lax.psum_scatter(
        part.astype(jnp.float32).astype(jnp.bfloat16), "col", scatter_dimension=0, tiled=True
    )
    return (output, grad_hidden, grad_weight.astype(jnp.bfloat16))


def solution(mesh):
    placed = (P("col", "row"), P("row", "col"), P("row", "col"))
    return jax.shard_map(
        per_device,
        mesh=mesh,
        in_specs=placed,
        out_specs=(P("row", "col"), P("col", "row"), P("row", "col")),
        check_vma=False,
    )
```

profile of v0, /device:TPU:1, one launch (start us, length us, event | category | flops | bytes accessed | tf_op | source)
XLA Modules:
  0.0 352.4 jit_solution(8082366088749023770)
XLA Ops:
  7.2 0.0 copy-start
  7.2 0.0 all-gather.5.cloned.1.call-start
  7.2 0.7 all-gather.5.cloned.1.call-update
  7.9 0.0 all-gather.3.cloned.1.call-start
  8.0 0.7 all-gather.3.cloned.1.call-update
  8.7 0.0 reduce-scatter.5.cloned.1.call-start
  8.7 56.3 %all-gather.5.cloned.1.call-done = bf16[2048,512]{1,0:T(8,128)(2,1)} async-done(((bf16[256,512]{1,0:T(8,128)(2,1)}), bf16[2048,512]{1,0:T(8,128)(2,1)}) %all-gather.5.cloned.1.call-update) | async-done | bytes 2097168 | tf_op jit(solution)/shard_map/all_gather | solution.py:8
  65.0 0.0 copy-done
  65.0 12.5 %convolution_convert_fusion = bf16[2048,3328]{1,0:T(8,128)(2,1)} fusion(bf16[2048,512]{1,0:T(8,128)(2,1)} %all-gather.5.cloned.1.call-done, bf16[3328,512]{1,0:T(8,128)(2,1)S(1)} %copy-done), kind=kOutput, calls=%fused_computation | convolution fusion | flops 6986137600 | bytes 19136512 | tf_op jit(solution)/shard_map/dot_general | solution.py:17
  77.5 0.0 reduce-scatter.5.cloned.1.call-update
  77.5 0.0 reduce-scatter.3.cloned.1.call-start
  77.6 85.4 %all-gather.3.cloned.1.call-done = bf16[2048,3328]{1,0:T(8,128)(2,1)} async-done(((bf16[128,3328]{1,0:T(8,128)(2,1)}), bf16[2048,3328]{1,0:T(8,128)(2,1)}) %all-gather.3.cloned.1.call-update) | async-done | bytes 13631504 | tf_op jit(solution)/shard_map/all_gather | solution.py:9
  162.9 11.3 %convolution_convert_fusion.2 = bf16[2048,512]{1,0:T(8,128)(2,1)} fusion(bf16[2048,3328]{1,0:T(8,128)(2,1)} %all-gather.3.cloned.1.call-done, bf16[3328,512]{1,0:T(8,128)(2,1)S(1)} %copy-done), kind=kOutput, calls=%fused_computation.2 | convolution fusion | flops 6980370432 | bytes 19136512 | tf_op jit(solution)/shard_map/dot_general | solution.py:10
  174.2 0.0 reduce-scatter.3.cloned.1.call-update
  174.2 15.8 %convolution_convert_fusion.1 = bf16[3328,512]{1,0:T(8,128)(2,1)} fusion(bf16[2048,3328]{1,0:T(8,128)(2,1)} %all-gather.3.cloned.1.call-done, bf16[2048,512]{1,0:T(8,128)(2,1)} %all-gather.5.cloned.1.call-done), kind=kOutput, calls=%fused_computation.1 | convolution fusion | flops 6981025792 | bytes 19136512 | tf_op jit(solution)/shard_map/dot_general | solution.py:11
  190.0 101.5 %reduce-scatter.5.cloned.1.call-done = bf16[128,3328]{1,0:T(8,128)(2,1)} async-done(((bf16[2048,3328]{1,0:T(8,128)(2,1)}), bf16[128,3328]{1,0:T(8,128)(2,1)}) %reduce-scatter.5.cloned.1.call-update) | async-done | bytes 851984 | tf_op jit(solution)/shard_map/reduce_scatter | solution.py:21
  291.6 54.3 %reduce-scatter.3.cloned.1.call-done = bf16[256,512]{1,0:T(8,128)(2,1)} async-done(((bf16[2048,512]{1,0:T(8,128)(2,1)}), bf16[256,512]{1,0:T(8,128)(2,1)}) %reduce-scatter.3.cloned.1.call-update) | async-done | bytes 262160 | tf_op jit(solution)/shard_map/reduce_scatter | solution.py:14
Async XLA Ops:
  7.2 57.9 %copy-start = (bf16[3328,512]{1,0:T(8,128)(2,1)S(1)}, bf16[3328,512]{1,0:T(8,128)(2,1)}, u32[]{:S(2)}) copy-start(bf16[3328,512]{1,0:T(8,128)(2,1)} %param.4) | copy-start | bytes 10223620
  7.2 57.8 %all-gather.5.cloned.1.call-start = ((), (), s32[]{:S(2)}) async-start(), calls=%async_computation.4 | async-start | bytes 2359296 | tf_op jit(solution)/shard_map/all_gather | solution.py:8
  7.9 155.0 %all-gather.3.cloned.1.call-start = ((), (), s32[]{:S(2)}) async-start(), calls=%async_computation.2 | async-start | bytes 14483456 | tf_op jit(solution)/shard_map/all_gather | solution.py:9
  8.7 282.9 %reduce-scatter.5.cloned.1.call-start = ((), (), s32[]{:S(2)}) async-start(), calls=%async_computation.5 | async-start | bytes 14483456 | tf_op jit(solution)/shard_map/reduce_scatter | solution.py:21
  77.5 268.3 %reduce-scatter.3.cloned.1.call-start = ((), (), s32[]{:S(2)}) async-start(), calls=%async_computation.3 | async-start | bytes 2359296 | tf_op jit(solution)/shard_map/reduce_scatter | solution.py:14
Sparse Core Ops, SparseCore 0:
  9.7 55.3 all-gather.4
  67.4 95.4 all-gather.2
  167.9 123.5 reduce-scatter.4
  294.4 51.3 reduce-scatter.2
where the time goes:
time: 352 us
  waiting for transfers between devices  299 us (85%)
  matrix products  39.6 us (11%)
  between operations  13.8 us (4%)
    reduce_scatter x1, waiting for transfers between devices, per_device(): lax.psum_scatter(part.astype(jnp.float32).astype(jnp.bfloat16), 'col', sc...  102 us
    all_gather x1, waiting for transfers between devices, per_device(): gathered = lax.all_gather(hidden, 'col', axis=0, tiled=True)  85.4 us
    all_gather x1, waiting for transfers between devices, per_device(): cotangents = lax.all_gather(grad_out, 'row', axis=0, tiled=True)  56.3 us
    reduce_scatter x1, waiting for transfers between devices, per_device(): lax.psum_scatter(partial_out.astype(jnp.bfloat16), 'row', scatter_dimensi...  54.3 us
    dot_general x1, matrix products, per_device(): lax.dot_general(gathered, cotangents, (((0,), (0,)), ((), ())), preferred...  15.8 us
    dot_general x1, matrix products, per_device(): lax.dot_general(cotangents, weight, (((1,), (1,)), ((), ())), preferred_e...  12.5 us
    dot_general x1, matrix products, per_device(): partial_out = jnp.dot(gathered, weight, preferred_element_type=jnp.float32)  11.3 us
  transfers between devices with their start and end apart: 4, of which 4 were waited for; matrix products, arithmetic and copies ran while one was open for 11% of the time, Pallas kernels for 0%

commit v1 on v0

--- a/solution.py
+++ b/solution.py
@@ -6,7 +6,9 @@
 
 def per_device(hidden, weight, grad_out):
     cotangents = lax.all_gather(grad_out, "row", axis=0, tiled=True)
-    gathered = lax.all_gather(hidden, "col", axis=0, tiled=True)
+    gathered = jnp.concatenate(
+        lax.all_to_all(jnp.stack([hidden] * lax.axis_size("col")), "col", 0, 0), axis=0
+    )
     partial_out = jnp.dot(gathered, weight, preferred_element_type=jnp.float32)
     grad_weight = lax.dot_general(
         gathered, cotangents, (((0,), (0,)), ((), ())), preferred_element_type=jnp.float32

time: 352 us -> 409 us (1.16)
  waiting for transfers between devices: 299 us -> 341 us
  starting transfers between devices: 0.16 us -> 8.56 us
  local copies, waits for them, and re-layouts: 0.01 us -> 7.54 us
    all_to_all x0 -> x1, waiting for transfers between devices: none -> 184 us  [per_device(): lax.all_to_all(jnp.stack([hidden] * lax.axis_size('col')), 'col', 0, 0)]
    all_gather x1 -> x0, waiting for transfers between devices: 85.4 us -> none  [per_device(): gathered = lax.all_gather(hidden, 'col', axis=0, tiled=True)]
    all_gather x1, waiting for transfers between devices: 56.3 us -> 0.02 us  [per_device(): cotangents = lax.all_gather(grad_out, 'row', axis=0, tiled=True)]
    reduce_scatter x1, waiting for transfers between devices: 102 us -> 131 us  [per_device(): lax.psum_scatter(part.astype(jnp.float32).astype(jnp.bfloat16), 'col', sc...]
    reduce_scatter x1, waiting for transfers between devices: 54.3 us -> 25.8 us  [per_device(): lax.psum_scatter(partial_out.astype(jnp.bfloat16), 'row', scatter_dimensi...]
    all_to_all x0 -> x1, starting transfers between devices: none -> 8.45 us  [per_device(): lax.all_to_all(jnp.stack([hidden] * lax.axis_size('col')), 'col', 0, 0)]
    another operation x0 -> x1, local copies, waits for them, and re-layouts: none -> 7.53 us  [per_device(): jnp.stack([hidden] * lax.axis_size('col'))]
  transfers between devices with their start and end apart: 4 -> 4, of which waited for: 4 -> 3; matrix products, arithmetic and copies ran while one was open for 11% -> 9% of each run, Pallas kernels for 0% -> 0%
where the time goes in v1:
time: 409 us; the launch traced here: 408 us
  waiting for transfers between devices  341 us (83%)
  matrix products  37.8 us (9%)
  between operations  13.8 us (3%)
  starting transfers between devices  8.56 us (2%)
  local copies, waits for them, and re-layouts  7.54 us (2%)
    all_to_all x1, waiting for transfers between devices, per_device(): lax.all_to_all(jnp.stack([hidden] * lax.axis_size('col')), 'col', 0, 0)  184 us
    reduce_scatter x1, waiting for transfers between devices, per_device(): lax.psum_scatter(part.astype(jnp.float32).astype(jnp.bfloat16), 'col', sc...  131 us
    reduce_scatter x1, waiting for transfers between devices, per_device(): lax.psum_scatter(partial_out.astype(jnp.bfloat16), 'row', scatter_dimensi...  25.8 us
    dot_general x1, matrix products, per_device(): lax.dot_general(gathered, cotangents, (((0,), (0,)), ((), ())), preferred...  14 us
    dot_general x1, matrix products, per_device(): lax.dot_general(cotangents, weight, (((1,), (1,)), ((), ())), preferred_e...  12.5 us
    dot_general x1, matrix products, per_device(): partial_out = jnp.dot(gathered, weight, preferred_element_type=jnp.float32)  11.3 us
    all_to_all x1, starting transfers between devices, per_device(): lax.all_to_all(jnp.stack([hidden] * lax.axis_size('col')), 'col', 0, 0)  8.45 us
  transfers between devices with their start and end apart: 4, of which 3 were waited for; matrix products, arithmetic and copies ran while one was open for 9% of the time, Pallas kernels for 0%

profile of v1, /device:TPU:1, one launch (start us, length us, event | category | flops | bytes accessed | tf_op | source)
XLA Modules:
  0.0 408.5 jit_solution(14596774663656578006)
XLA Ops:
  7.2 0.0 copy-start
  7.2 7.5 %stack.2 = bf16[16,128,3328]{2,1,0:T(8,128)(2,1)} broadcast(bf16[128,3328]{1,0:T(8,128)(2,1)} %param.3), dimensions={1,2} | broadcast | bytes 14483456 | tf_op jit(solution)/shard_map/stack | solution.py:10
  14.7 8.4 %all-to-all-start = ((bf16[16,128,3328]{2,1,0:T(8,128)(2,1)}), bf16[16,128,3328]{2,1,0:T(8,128)(2,1)}, u32[]{:S(2)}, u32[]{:S(2)}) async-start(bf16[16,128,3328]{2,1,0:T(8,128)(2,1)} %stack.2), calls=%async_computation | async-start | bytes 27262976 | tf_op jit(solution)/shard_map/all_to_all | solution.py:10
  23.2 0.0 all-gather.2.cloned.1.call-start
  23.2 0.7 all-gather.2.cloned.1.call-update
  23.9 0.0 reduce-scatter.3.cloned.1.call-start
  23.9 183.8 %all-to-all-done = bf16[16,128,3328]{2,1,0:T(8,128)(2,1)} async-done(((bf16[16,128,3328]{2,1,0:T(8,128)(2,1)}), bf16[16,128,3328]{2,1,0:T(8,128)(2,1)}, u32[]{:S(2)}, u32[]{:S(2)}) %all-to-all-start) | async-done | bytes 13631520 | tf_op jit(solution)/shard_map/all_to_all | solution.py:10
  207.7 0.0 copy-done
  207.7 11.3 %convolution_convert_fusion.2 = bf16[2048,512]{1,0:T(8,128)(2,1)} fusion(bf16[2048,3328]{1,0:T(8,128)(2,1)} %bitcast, bf16[3328,512]{1,0:T(8,128)(2,1)S(1)} %copy-done), kind=kOutput, calls=%fused_computation.2 | convolution fusion | flops 6980370432 | bytes 19136512 | tf_op jit(solution)/shard_map/dot_general | solution.py:12
  219.0 0.0 reduce-scatter.3.cloned.1.call-update
  219.0 0.0 reduce-scatter.5.cloned.1.call-start
  219.0 0.0 all-gather.2.cloned.1.call-done
  219.1 12.5 %convolution_convert_fusion = bf16[2048,3328]{1,0:T(8,128)(2,1)} fusion(bf16[2048,512]{1,0:T(8,128)(2,1)} %all-gather.2.cloned.1.call-done, bf16[3328,512]{1,0:T(8,128)(2,1)S(1)} %copy-done), kind=kOutput, calls=%fused_computation | convolution fusion | flops 6986137600 | bytes 19136512 | tf_op jit(solution)/shard_map/dot_general | solution.py:19
  231.6 0.0 reduce-scatter.5.cloned.1.call-update
  231.6 14.0 %convolution_convert_fusion.1 = bf16[3328,512]{1,0:T(8,128)(2,1)} fusion(bf16[2048,3328]{1,0:T(8,128)(2,1)} %bitcast, bf16[2048,512]{1,0:T(8,128)(2,1)} %all-gather.2.cloned.1.call-done), kind=kOutput, calls=%fused_computation.1 | convolution fusion | flops 6981025792 | bytes 19136512 | tf_op jit(solution)/shard_map/dot_general | solution.py:13
  245.6 25.8 %reduce-scatter.3.cloned.1.call-done = bf16[256,512]{1,0:T(8,128)(2,1)} async-done(((bf16[2048,512]{1,0:T(8,128)(2,1)}), bf16[256,512]{1,0:T(8,128)(2,1)}) %reduce-scatter.3.cloned.1.call-update) | async-done | bytes 262160 | tf_op jit(solution)/shard_map/reduce_scatter | solution.py:16
  271.4 130.5 %reduce-scatter.5.cloned.1.call-done = bf16[128,3328]{1,0:T(8,128)(2,1)} async-done(((bf16[2048,3328]{1,0:T(8,128)(2,1)}), bf16[128,3328]{1,0:T(8,128)(2,1)}) %reduce-scatter.5.cloned.1.call-update) | async-done | bytes 851984 | tf_op jit(solution)/shard_map/reduce_scatter | solution.py:23
Async XLA Ops:
  7.2 200.5 %copy-start = (bf16[3328,512]{1,0:T(8,128)(2,1)S(1)}, bf16[3328,512]{1,0:T(8,128)(2,1)}, u32[]{:S(2)}) copy-start(bf16[3328,512]{1,0:T(8,128)(2,1)} %param.4) | copy-start | bytes 10223620
  14.7 193.0 %all-to-all-start = ((bf16[16,128,3328]{2,1,0:T(8,128)(2,1)}), bf16[16,128,3328]{2,1,0:T(8,128)(2,1)}, u32[]{:S(2)}, u32[]{:S(2)}) async-start(bf16[16,128,3328]{2,1,0:T(8,128)(2,1)} %stack.2), calls=%async_computation | async-start | bytes 27262976 | tf_op jit(solution)/shard_map/all_to_all | solution.py:10
  23.2 195.9 %all-gather.2.cloned.1.call-start = ((), (), s32[]{:S(2)}) async-start(), calls=%async_computation.4 | async-start | bytes 2359296 | tf_op jit(solution)/shard_map/all_gather | solution.py:8
  23.9 247.5 %reduce-scatter.3.cloned.1.call-start = ((), (), s32[]{:S(2)}) async-start(), calls=%async_computation.3 | async-start | bytes 2359296 | tf_op jit(solution)/shard_map/reduce_scatter | solution.py:16
  219.0 182.9 %reduce-scatter.5.cloned.1.call-start = ((), (), s32[]{:S(2)}) async-start(), calls=%async_computation.5 | async-start | bytes 14483456 | tf_op jit(solution)/shard_map/reduce_scatter | solution.py:23
Sparse Core Ops, SparseCore 0:
  25.6 188.0 all-gather.1
  219.1 52.2 reduce-scatter.2
  276.4 125.4 reduce-scatter.4
